TPU v7x, 512 devices: a whole 4x4x16 slice. The times are simulated.
512 devices in a mesh: replica: 8 (over z_hi, core), fsdp: 64 (over y, z_lo, x).
Axes of the slice: x: 4, y: 4, z: 16 (z_hi: 4, z_lo: 4; z = z_hi * 4 + z_lo), core: 2. Of those that a mesh axis runs over, the one named last changes fastest.
Arguments:
- inputs: bfloat16 [12288, 8192], P('fsdp'), may hold values from -6 to 6
- local_weights: float32 [8, 512, 8192], P('replica', 'fsdp'), may hold values from -8 to 8
- global_base: float32 [512, 8192], P('fsdp'), may hold values from -4 to 4
- momentum: float32 [512, 8192], P('fsdp'), may hold values from -3 to 3
Outputs:
- new_base: float32 [512, 8192], P('fsdp')
- new_momentum: float32 [512, 8192], P('fsdp')
- keys: bfloat16 [12288, 512], P('fsdp')
All inputs are finite; a program needn't handle non-finite values.
Results may differ from a plain program's by a relative error of at most 0.014.
Values may be sent and summed in bfloat16 or wider, within the bound.
A program may use at most 64 MiB of HBM per device.

v0:
```python
import jax
import jax.numpy as jnp
from jax import lax
from jax.sharding import PartitionSpec as P

QBLOCK = 128


EPSILON = 1e-06
CODE_RANGE = 127.0
OUTER_RATE = 0.7
OUTER_MOMENTUM = 0.9


def nesterov(outer_grad, global_base, momentum):
    new_momentum = OUTER_MOMENTUM * momentum + outer_grad
    new_base = global_base - OUTER_RATE * (outer_grad + OUTER_MOMENTUM * new_momentum)
    return (new_base, new_momentum)


def shards(inputs, local_weights, global_base, momentum):
    frag_rows = global_base.shape[0]
    width = global_base.shape[1]
    replica_count = lax.axis_size("replica")
    pseudo_grad = global_base - local_weights[0]
    blocks = pseudo_grad.reshape(frag_rows, width // QBLOCK, QBLOCK)
    block_max = jnp.max(jnp.abs(blocks), axis=-1)
    block_scale = jnp.exp2(jnp.ceil(jnp.log2((block_max + EPSILON) / CODE_RANGE))).astype(
        jnp.bfloat16
    )
    quant_codes = jnp.floor(blocks / block_scale.astype(jnp.float32)[..., None] + 0.5).astype(
        jnp.bfloat16
    )
    restored = quant_codes.astype(jnp.float32) * block_scale.astype(jnp.float32)[..., None]
    summed = lax.psum(restored.reshape(frag_rows, width).astype(jnp.bfloat16), "replica").astype(
        jnp.float32
    )
    new_base, new_momentum = nesterov(summed / replica_count, global_base, momentum)
    weight = new_base.astype(jnp.bfloat16)
    key_acc = lax.dot_general(
        inputs,
        lax.all_gather(weight, "fsdp", axis=0, tiled=True),
        (((1,), (1,)), ((), ())),
        preferred_element_type=jnp.float32,
    )
    keys = key_acc.astype(jnp.bfloat16)
    return (new_base, new_momentum, keys)


def solution(mesh):
    return jax.shard_map(
        shards,
        mesh=mesh,
        in_specs=(P("fsdp", None), P("replica", "fsdp", None), P("fsdp", None), P("fsdp", None)),
        out_specs=(P("fsdp", None), P("fsdp", None), P("fsdp", None)),
        check_vma=False,
    )
```

profile of v0, /device:TPU:2, one launch (start us, length us, event | category | flops | bytes accessed | tf_op | source)
XLA Modules:
  0.0 490.7 jit_solution(13166764779246980569)
XLA Ops:
  7.2 0.0 copy-start
  7.2 0.0 all-reduce.2.cloned.1.call-start
  7.2 1.3 bitcast_reduce_fusion
  8.6 0.1 copy.8
  8.6 0.1 copy.9
  8.7 1.8 fusion.4
  10.6 0.0 all-reduce.2.cloned.1.call-update
  10.6 0.0 all-gather.2.cloned.1.call-start
  10.6 101.7 %all-reduce.2.cloned.1.call-done = bf16[8,8192]{1,0:T(8,128)(2,1)} async-done(((bf16[8,8192]{1,0:T(8,128)(2,1)}), bf16[8,8192]{1,0:T(8,128)(2,1)}) %all-reduce.2.cloned.1.call-update) | async-done | bytes 131088 | tf_op jit(solution)/shard_map/psum | solution.py:35
  112.3 2.0 fusion.6
  114.3 0.0 all-gather.2.cloned.1.call-update
  114.4 362.5 %all-gather.2.cloned.1.call-done = bf16[512,8192]{1,0:T(8,128)(2,1)} async-done(((bf16[8,8192]{1,0:T(8,128)(2,1)}), bf16[512,8192]{1,0:T(8,128)(2,1)}) %all-gather.2.cloned.1.call-update) | async-done | bytes 8388624 | tf_op jit(solution)/shard_map/all_gather | solution.py:42
  476.9 0.0 copy-done
  476.9 7.0 %fusion = bf16[192,512]{1,0:T(8,128)(2,1)} fusion(bf16[512,8192]{1,0:T(8,128)(2,1)} %all-gather.2.cloned.1.call-done, bf16[192,8192]{1,0:T(8,128)(2,1)S(1)} %copy-done), kind=kOutput, calls=%fused_computation.1 | convolution fusion | flops 1610711040 | bytes 11730944 | tf_op jit(solution)/shard_map/dot_general | solution.py:40
  (1 shorter events, 0.0 us)
Async XLA Ops:
  7.2 469.7 %copy-start = (bf16[192,8192]{1,0:T(8,128)(2,1)S(1)}, bf16[192,8192]{1,0:T(8,128)(2,1)}, u32[]{:S(2)}) copy-start(bf16[192,8192]{1,0:T(8,128)(2,1)} %param.4) | copy-start | bytes 9437188
  7.2 105.2 %all-reduce.2.cloned.1.call-start = ((), (), s32[]{:S(2)}) async-start(), calls=%async_computation | async-start | bytes 262144 | tf_op jit(solution)/shard_map/psum | solution.py:35
  10.6 466.3 %all-gather.2.cloned.1.call-start = ((), (), s32[]{:S(2)}) async-start(), calls=%async_computation.1 | async-start | bytes 8519680 | tf_op jit(solution)/shard_map/all_gather | solution.py:42
Sparse Core Ops, SparseCore 0:
  11.5 100.8 all-reduce.1
  115.2 361.6 all-gather.1
where the time goes:
time: 491 us
  waiting for transfers between devices  464 us (95%)
  between operations  14.1 us (3%)
  matrix products  6.96 us (1%)
  other arithmetic  5.18 us (1%)
    all_gather x1, waiting for transfers between devices, shards(): lax.all_gather(weight, 'fsdp', axis=0, tiled=True)  363 us
    psum x1, waiting for transfers between devices, shards(): lax.psum(restored.reshape(frag_rows, width).astype(jnp.bfloat16), 'replica')  102 us
  transfers between devices with their start and end apart: 2, of which 2 were waited for; matrix products, arithmetic and copies ran while one was open for 0% of the time, Pallas kernels for 0%

commit v1 on v0

v1 whole, which is shorter than its diff:
```python
import jax
import jax.numpy as jnp
from jax import lax
from jax.experimental import pallas as pl
from jax.experimental.pallas import tpu as pltpu
from jax.sharding import PartitionSpec as P

MESH = pl.DeviceIdType.MESH
F32, BF16 = jnp.float32, jnp.bfloat16
EPSILON = 1e-06
CODE_RANGE = 127.0
OUTER_RATE = 0.7
OUTER_MOMENTUM = 0.9
QBLOCK = 128
BLOCKS = 64
ROWS = 8
HALF = 32
SLOTS = 64
TOKENS = 192
PACKED = TOKENS // 2


def rem(a, b):
    return lax.rem(a, jnp.int32(b))


def div(a, b):
    return lax.div(a, jnp.int32(b))


def device(z, core, y, x):
    return (2 * div(z, 4) + core, 16 * y + 4 * rem(z, 4) + x)


def parity(x, y):
    return 1 - 2 * rem(x + y, 2)


def rows(start, count):
    return pl.ds(pl.multiple_of(start, count), count)


def kernel(
    inp, lw, base, mom, nb_out, nm_out, keys_out,
    lw_v, base_v, mom_v, x_v, spread, core_send, core_recv, far_send, far_recv, lead_send, lead_recv,
    pieces, turned, weight, og_own, og_recv, og_other, part, perm, keys_v,
    load_sem, core_sem, far_ssem, far_rsem, lead_sem, piece_ssem, piece_rsem, og_ssem, og_rsem, ogc_sem,
    key_ssem, key_rsem, out_sem,
):
    replica = lax.axis_index("replica")
    fsdp = lax.axis_index("fsdp")
    z_hi, core = div(replica, 2), rem(replica, 2)
    y, z_lo, x = div(fsdp, 16), rem(div(fsdp, 4), 4), rem(fsdp, 4)
    z = 4 * z_hi + z_lo
    mine = parity(x, y)

    def at(dz=0, dy=0, dx=0, other=False):
        return device(
            rem(z + dz + 16, 16), 1 - core if other else core, rem(y + dy, 4), rem(x + dx, 4)
        )

    def remote(src, dst, ssem, rsem, to):
        return pltpu.make_async_remote_copy(
            src_ref=src, dst_ref=dst, send_sem=ssem, recv_sem=rsem, device_id=to, device_id_type=MESH
        )

    loads = [
        pltpu.make_async_copy(lw, lw_v, load_sem.at[0]),
        pltpu.make_async_copy(base, base_v, load_sem.at[1]),
        pltpu.make_async_copy(mom, mom_v, load_sem.at[2]),
        pltpu.make_async_copy(inp, x_v, load_sem.at[3]),
    ]
    for load in loads:
        load.start()

    barrier = pltpu.get_barrier_semaphore()
    greeted = 0

    def greet(to):
        pl.semaphore_signal(barrier, inc=1, device_id=to, device_id_type=MESH)

    for dz in (6, -6, 2, -2):
        greet(at(dz))
        greeted += 1
    for dx in range(4):
        there = parity(rem(x + dx, 4), y)
        for dz in (0, 1, -1, None):
            if dx or dz != 0:
                greet(at(-2 * there if dz is None else -dz, 0, dx))
                greeted += 1
    for dy in range(1, 4):
        there = parity(x, rem(y + dy, 4))
        for dz in (0, 1, -1, None):
            greet(at(-2 * there if dz is None else -dz, dy))
            greeted += 1
    greet(at(other=True))
    greeted += 1

    loads[0].wait()
    loads[1].wait()

    def quantize(step, carry):
        for k in range(4):
            b = step * 4 + k
            columns = rows(b * QBLOCK, QBLOCK)
            pseudo = base_v[:, columns] - lw_v[:, columns]
            peak = jnp.max(jnp.abs(pseudo), axis=-1, keepdims=True)
            scale = jnp.exp2(jnp.ceil(jnp.log2((peak + EPSILON) / CODE_RANGE)))
            scale = scale.astype(BF16).astype(F32)
            codes = jnp.floor(pseudo / scale + 0.5).astype(BF16).astype(F32)
            spread[rows(b * ROWS, ROWS), :] = codes * scale
        return carry

    lax.fori_loop(0, BLOCKS // 4, quantize, 0)

    def row(ref, q):
        return ref[pl.ds(q, BLOCKS, stride=ROWS), :]

    for k in range(4):
        core_send[k * BLOCKS : (k + 1) * BLOCKS, :] = row(spread, 2 * k + 1 - core).astype(BF16)

    pl.semaphore_wait(barrier, greeted)

    swap = remote(core_send, core_recv, core_sem.at[0], core_sem.at[1], at(other=True))
    swap.start()

    loads[2].wait()
    lead_q = 2 * div(rem(z + 2, 16), 4) + core
    keep = [row(spread, 2 * k + core) for k in range(4)]

    def lead_rows(step, carry):
        for k in range(4):
            b = step * 4 + k
            columns = rows(b * QBLOCK, QBLOCK)
            turned[rows(b * ROWS, ROWS), :] = base_v[:, columns] - (
                OUTER_RATE * OUTER_MOMENTUM * OUTER_MOMENTUM
            ) * mom_v[:, columns]
        return carry

    lax.fori_loop(0, BLOCKS // 4, lead_rows, 0)
    lead_send[...] = row(turned, lead_q)

    swap.wait_recv()
    for k in range(4):
        part_sum = keep[k] + core_recv[k * BLOCKS : (k + 1) * BLOCKS, :].astype(F32)
        far_send[k * BLOCKS : (k + 1) * BLOCKS, :] = part_sum.astype(BF16)
    fars = []
    for j, dz in enumerate((6, -6, 2, -2)):
        k = div(rem(z + dz + 16, 16), 4)
        fars.append(
            remote(
                far_send.at[rows(k * BLOCKS, BLOCKS)],
                far_recv.at[pl.ds(j * BLOCKS, BLOCKS)],
                far_ssem.at[j],
                far_rsem.at[j],
                at(dz),
            )
        )
        fars[-1].start()
    lead = remote(lead_send, lead_recv, lead_sem.at[0], lead_sem.at[1], at(2))
    lead.start()

    def order(j, carry):
        late = jnp.where(j >= 6, 1, 0)
        other = late * (j - 6) + (1 - late) * div(j, 3)
        turn = late * 2 + (1 - late) * rem(j * j, 3) * (1 + 2 * jnp.where(rem(j, 3) == 2, 1, 0))
        there_hi = z_hi + turn
        there_core = rem(core + other, 2)
        line = lax.broadcasted_iota(jnp.int32, (128, QBLOCK), 0)
        slot = line % SLOTS
        step = (z_lo + 2 - (slot // 4) % 4 + 4) % 4
        sign = 1 - 2 * ((slot % 4 + slot // 16) % 2)
        dz = jnp.where(step == 2, 2 * sign, jnp.where(step == 3, -1, step))
        source = (4 * there_hi + z_lo - dz + 32) % 16
        target = 8 * slot + 2 * (source // 4) + there_core
        lane = lax.broadcasted_iota(jnp.int32, (128, QBLOCK), 1)
        for half in range(2):
            wanted = jnp.where(line // SLOTS == half, target, -1)
            for n in range(4):
                hit = jnp.where(wanted == lane + n * QBLOCK, 1.0, 0.0).astype(BF16)
                first = half * 512 + n * QBLOCK
                perm[rows(j * 128, 128), first : first + QBLOCK] = hit
        return carry

    lax.fori_loop(0, 8, order, 0)

    for far in fars:
        far.wait_recv()
    lead.wait_recv()
    total = jnp.zeros((BLOCKS, QBLOCK), F32)
    for j in range(4):
        total += far_recv[j * BLOCKS : (j + 1) * BLOCKS, :].astype(F32)
    grad = total * 0.125
    gain = OUTER_RATE * (1.0 + OUTER_MOMENTUM)
    new_row = (lead_recv[...] - gain * grad).astype(BF16)
    own_class = rem(z + 2, 4)

    def place(half, slot):
        return rows((half * SLOTS + slot) * HALF, HALF)

    own_slot = 16 * y + 4 * own_class + x
    pieces[place(0, own_slot), :] = new_row[:HALF]
    pieces[place(1, own_slot), :] = new_row[HALF:]

    def send_piece(half, slot, to):
        spot = pieces.at[place(half, slot)]
        remote(spot, spot, piece_ssem, piece_rsem.at[half * SLOTS + slot], to).start()

    def turn_piece(half, slot):
        turned[pl.ds(half * HALF * SLOTS + slot, HALF, stride=SLOTS), :] = pieces[
            place(half, slot), :
        ].astype(F32)

    def wait_piece(half, slot):
        spot = pieces.at[place(half, slot)]
        remote(spot, spot, piece_ssem, piece_rsem.at[half * SLOTS + slot], at(2)).wait_recv()

    steps = [(a, b) for a in range(4) for b in range(4)]
    length = [0, 1, 2, 1]
    steps.sort(key=lambda s: length[s[0]] + length[s[1]])
    for a, b in reversed(steps):
        dz = (0, 1, 2 * mine, -1)[b]
        if a or b:
            send_piece(0, own_slot, at(dz, 0, a))
            send_piece(1, own_slot, at(dz, a, 0))
    og_own[...] = grad.astype(BF16)

    for a, b in steps:
        for half in range(2):
            px, py = (rem(x + a, 4), y) if half == 0 else (x, rem(y + a, 4))
            there = parity(px, py)
            dz = (0, -1, -2 * there, 1)[b]
            kind = rem(z + dz + 16 + 2, 4)
            slot = 16 * py + 4 * kind + px
            if a or b:
                wait_piece(half, slot)
            for d in (2, 1, 3):
                send_piece(half, slot, at(0, d, 0) if half == 0 else at(0, 0, d))
            turn_piece(half, slot)

    ogs = []
    for j, dz in enumerate((6, -6, 2, -2)):
        ogs.append(
            remote(og_own, og_recv.at[rows(z_hi * BLOCKS, BLOCKS)], og_ssem.at[j], og_rsem.at[z_hi], at(dz))
        )
        ogs[-1].start()

    loads[3].wait()
    def second(i, carry):
        kind, p = div(i, 4), rem(i, 4)
        for d in (1, 3, 2):
            for half in range(2):
                if half == 0:
                    slot = 16 * rem(y + d, 4) + 4 * kind + p
                else:
                    slot = 16 * p + 4 * kind + rem(x + d, 4)
                wait_piece(half, slot)
                turn_piece(half, slot)
        return carry

    lax.fori_loop(0, 16, second, 0)

    for b in range(BLOCKS):
        weight[:, b * QBLOCK : (b + 1) * QBLOCK] = turned[b * SLOTS : (b + 1) * SLOTS, :].astype(BF16)
    keys = lax.dot_general(
        x_v[...], weight[...], (((1,), (1,)), ((), ())), preferred_element_type=F32
    ).astype(BF16)
    part[:, 0:QBLOCK] = jnp.concatenate([keys[:PACKED], keys[PACKED:]], axis=1)

    def spot(j):
        return part.at[:, pl.ds(j * QBLOCK, QBLOCK)]

    sends = []

    def send_keys(j, to_j, to):
        copy = remote(spot(j), spot(to_j), key_ssem.at[len(sends)], key_rsem.at[to_j], to)
        copy.start()
        sends.append(copy)

    def wait_keys(j):
        remote(spot(0), spot(j), key_ssem.at[0], key_rsem.at[j], at(2)).wait_recv()

    send_keys(0, 6, at(8))
    send_keys(0, 2, at(4))
    send_keys(0, 1, at(-4))
    send_keys(0, 3, at(other=True))

    for k in range(4):
        home = og_recv.at[pl.ds(k * BLOCKS, BLOCKS)]
        remote(home, home, og_ssem.at[0], og_rsem.at[k], at(2)).wait_recv()
    relay = remote(og_recv, og_other, ogc_sem.at[0], ogc_sem.at[1], at(other=True))
    relay.start()
    relay.wait_recv()
    for k in range(4):
        span = slice(k * BLOCKS, (k + 1) * BLOCKS)
        spread[pl.ds(2 * k + core, BLOCKS, stride=ROWS), :] = og_recv[span, :].astype(F32)
        spread[pl.ds(2 * k + 1 - core, BLOCKS, stride=ROWS), :] = og_other[span, :].astype(F32)

    def outer(step, carry):
        for k in range(4):
            b = step * 4 + k
            columns = rows(b * QBLOCK, QBLOCK)
            og = spread[rows(b * ROWS, ROWS), :]
            new_momentum = OUTER_MOMENTUM * mom_v[:, columns] + og
            base_v[:, columns] = base_v[:, columns] - OUTER_RATE * (og + OUTER_MOMENTUM * new_momentum)
            mom_v[:, columns] = new_momentum
        return carry

    lax.fori_loop(0, BLOCKS // 4, outer, 0)
    stores = [
        pltpu.make_async_copy(base_v, nb_out, out_sem.at[0]),
        pltpu.make_async_copy(mom_v, nm_out, out_sem.at[1]),
    ]
    for store in stores:
        store.start()

    for j in (1, 2):
        wait_keys(j)
        send_keys(j, j + 3, at(other=True))
    for j in (3, 4, 5):
        wait_keys(j)

    def ordered(first, last):
        held = part[:, first * QBLOCK : last * QBLOCK]
        table = perm[first * QBLOCK : last * QBLOCK, :]
        return jnp.dot(held, table, preferred_element_type=F32)

    early = ordered(0, 6)
    wait_keys(6)
    send_keys(6, 7, at(other=True))
    wait_keys(7)
    done = (early + ordered(6, 8)).astype(BF16)
    keys_v[:PACKED, :] = done[:, :512]
    keys_v[PACKED:, :] = done[:, 512:]
    stores.append(pltpu.make_async_copy(keys_v, keys_out, out_sem.at[2]))
    stores[-1].start()

    swap.wait_send()
    lead.wait_send()
    relay.wait_send()
    for copy in fars + ogs + sends:
        copy.wait_send()
    sent = pieces.at[pl.ds(0, (30 + 96) * HALF)]
    remote(sent, sent, piece_ssem, piece_rsem.at[0], at(2)).wait_send()
    for store in stores:
        store.wait()


def shards(inputs, local_weights, global_base, momentum):
    width = global_base.shape[1]
    shape = jax.ShapeDtypeStruct
    dma = pltpu.SemaphoreType.DMA
    return pl.pallas_call(
        kernel,
        name="outer_step_and_keys",
        out_shape=(
            shape((ROWS, width), F32),
            shape((ROWS, width), F32),
            shape((TOKENS, 512), BF16),
        ),
        in_specs=[pl.BlockSpec(memory_space=pl.ANY)] * 4,
        out_specs=[pl.BlockSpec(memory_space=pl.ANY)] * 3,
        scratch_shapes=[
            pltpu.VMEM((ROWS, width), F32),
            pltpu.VMEM((ROWS, width), F32),
            pltpu.VMEM((ROWS, width), F32),
            pltpu.VMEM((TOKENS, width), BF16),
            pltpu.VMEM((BLOCKS * ROWS, QBLOCK), F32),
            pltpu.VMEM((4 * BLOCKS, QBLOCK), BF16),
            pltpu.VMEM((4 * BLOCKS, QBLOCK), BF16),
            pltpu.VMEM((4 * BLOCKS, QBLOCK), BF16),
            pltpu.VMEM((4 * BLOCKS, QBLOCK), BF16),
            pltpu.VMEM((BLOCKS, QBLOCK), F32),
            pltpu.VMEM((BLOCKS, QBLOCK), F32),
            pltpu.VMEM((SLOTS * BLOCKS, QBLOCK), BF16),
            pltpu.VMEM((SLOTS * BLOCKS, QBLOCK), F32),
            pltpu.VMEM((SLOTS, width), BF16),
            pltpu.VMEM((BLOCKS, QBLOCK), BF16),
            pltpu.VMEM((4 * BLOCKS, QBLOCK), BF16),
            pltpu.VMEM((4 * BLOCKS, QBLOCK), BF16),
            pltpu.VMEM((PACKED, 8 * QBLOCK), BF16),
            pltpu.VMEM((8 * QBLOCK, 1024), BF16),
            pltpu.VMEM((TOKENS, 512), BF16),
            dma((4,)),
            dma((2,)),
            dma((4,)),
            dma((4,)),
            dma((2,)),
            dma,
            dma((2 * SLOTS,)),
            dma((4,)),
            dma((4,)),
            dma((2,)),
            dma((7,)),
            dma((8,)),
            dma((3,)),
        ],
        compiler_params=pltpu.CompilerParams(
            collective_id=0, has_side_effects=True, vmem_limit_bytes=62 * 2**20
        ),
        cost_estimate=pl.CostEstimate(flops=2 * 192 * 64 * 8192, bytes_accessed=5 * 2**20, transcendentals=1024),
    )(inputs, local_weights.reshape(ROWS, width), global_base, momentum)


def solution(mesh):
    return jax.shard_map(
        shards,
        mesh=mesh,
        in_specs=(P("fsdp", None), P("replica", "fsdp", None), P("fsdp", None), P("fsdp", None)),
        out_specs=(P("fsdp", None), P("fsdp", None), P("fsdp", None)),
        check_vma=False,
    )
```

time: 491 us -> 58.4 us (0.12)
  the two profiles are of different devices: /device:TPU:2 before, /device:TPU:1 now
where the time goes in v1:
time: 58.4 us; the launch traced here: 57.4 us
  Pallas kernels  51.9 us (89%)
  local copies, waits for them, and re-layouts  4.95 us (8%)
  between operations  0.64 us (1%)
    pallas_call x1, Pallas kernels, shards(): pl.pallas_call(kernel, name='outer_step_and_keys', out_shape=(shape((ROWS...  51.9 us
    unnamed x3, local copies, waits for them, and re-layouts  4.95 us

profile of v1, /device:TPU:1, one launch (start us, length us, event | category | flops | bytes accessed | tf_op | source)
XLA Modules:
  0.0 57.4 jit_solution(9992988748593763730)
XLA Ops:
  0.6 51.9 %outer_step_and_keys.1 = (f32[8,8192]{1,0:T(8,128)}, f32[8,8192]{1,0:T(8,128)}, bf16[192,512]{1,0:T(8,128)(2,1)}) custom-call(bf16[192,8192]{1,0:T(8,128)(2,1)} %inp.1, f32[8,8192]{1,0:T(8,128)} %bitcast.1, f32[8,8192]{1,0:T(8,128)} %base.1, f32[8,8192]{1,0:T(8,128)} %mom.1), custom_call_target="tpu_custom_call" | custom-call | flops 201326592 | bytes 5242880 | tf_op jit(solution)/shard_map/outer_step_and_keys/pallas_call | solution.py:353
  52.5 1.7 %copy.10 = f32[8,8192]{1,0:T(8,128)} copy(f32[8,8192]{1,0:T(8,128)} %get-tuple-element.6) | data formatting | bytes 524288
  54.2 1.7 %copy.11 = f32[8,8192]{1,0:T(8,128)} copy(f32[8,8192]{1,0:T(8,128)} %get-tuple-element.7) | data formatting | bytes 524288
  55.8 1.6 %copy.12 = bf16[192,512]{1,0:T(8,128)(2,1)} copy(bf16[192,512]{1,0:T(8,128)(2,1)} %get-tuple-element.8) | data formatting | bytes 393216

commit v2 on v1

--- a/solution.py
+++ b/solution.py
@@ -43,9 +43,9 @@
 def kernel(
     inp, lw, base, mom, nb_out, nm_out, keys_out,
     lw_v, base_v, mom_v, x_v, spread, core_send, core_recv, far_send, far_recv, lead_send, lead_recv,
-    pieces, turned, weight, og_own, og_recv, og_other, part, perm, keys_v,
+    pieces, turned, weight, og_own, og_recv, og_other, part, perm,
     load_sem, core_sem, far_ssem, far_rsem, lead_sem, piece_ssem, piece_rsem, og_ssem, og_rsem, ogc_sem,
-    key_ssem, key_rsem, out_sem,
+    key_ssem, key_rsem,
 ):
     replica = lax.axis_index("replica")
     fsdp = lax.axis_index("fsdp")
@@ -218,7 +218,7 @@
     steps = [(a, b) for a in range(4) for b in range(4)]
     length = [0, 1, 2, 1]
     steps.sort(key=lambda s: length[s[0]] + length[s[1]])
-    for a, b in reversed(steps):
+    for a, b in steps:
         dz = (0, 1, 2 * mine, -1)[b]
         if a or b:
             send_piece(0, own_slot, at(dz, 0, a))
@@ -302,18 +302,11 @@
             columns = rows(b * QBLOCK, QBLOCK)
             og = spread[rows(b * ROWS, ROWS), :]
             new_momentum = OUTER_MOMENTUM * mom_v[:, columns] + og
-            base_v[:, columns] = base_v[:, columns] - OUTER_RATE * (og + OUTER_MOMENTUM * new_momentum)
-            mom_v[:, columns] = new_momentum
+            nb_out[:, columns] = base_v[:, columns] - OUTER_RATE * (og + OUTER_MOMENTUM * new_momentum)
+            nm_out[:, columns] = new_momentum
         return carry
 
     lax.fori_loop(0, BLOCKS // 4, outer, 0)
-    stores = [
-        pltpu.make_async_copy(base_v, nb_out, out_sem.at[0]),
-        pltpu.make_async_copy(mom_v, nm_out, out_sem.at[1]),
-    ]
-    for store in stores:
-        store.start()
-
     for j in (1, 2):
         wait_keys(j)
         send_keys(j, j + 3, at(other=True))
@@ -330,10 +323,8 @@
     send_keys(6, 7, at(other=True))
     wait_keys(7)
     done = (early + ordered(6, 8)).astype(BF16)
-    keys_v[:PACKED, :] = done[:, :512]
-    keys_v[PACKED:, :] = done[:, 512:]
-    stores.append(pltpu.make_async_copy(keys_v, keys_out, out_sem.at[2]))
-    stores[-1].start()
+    keys_out[:PACKED, :] = done[:, :512]
+    keys_out[PACKED:, :] = done[:, 512:]
 
     swap.wait_send()
     lead.wait_send()
@@ -342,24 +333,37 @@
         copy.wait_send()
     sent = pieces.at[pl.ds(0, (30 + 96) * HALF)]
     remote(sent, sent, piece_ssem, piece_rsem.at[0], at(2)).wait_send()
-    for store in stores:
-        store.wait()
+
+
+def store(nb, nm, keys, nb_out, nm_out, keys_out, sem):
+    copies = [
+        pltpu.make_async_copy(here, there, sem.at[j])
+        for j, (here, there) in enumerate(((keys, keys_out), (nb, nb_out), (nm, nm_out)))
+    ]
+    for copy in copies:
+        copy.start()
+    for copy in copies:
+        copy.wait()
 
 
 def shards(inputs, local_weights, global_base, momentum):
     width = global_base.shape[1]
     shape = jax.ShapeDtypeStruct
     dma = pltpu.SemaphoreType.DMA
-    return pl.pallas_call(
+    inputs, local_weights, global_base, momentum = (
+        pltpu.with_memory_space_constraint(a, pltpu.HBM)
+        for a in (inputs, local_weights.reshape(ROWS, width), global_base, momentum)
+    )
+    results = pl.pallas_call(
         kernel,
         name="outer_step_and_keys",
         out_shape=(
-            shape((ROWS, width), F32),
-            shape((ROWS, width), F32),
-            shape((TOKENS, 512), BF16),
+            pltpu.VMEM((ROWS, width), F32),
+            pltpu.VMEM((ROWS, width), F32),
+            pltpu.VMEM((TOKENS, 512), BF16),
         ),
         in_specs=[pl.BlockSpec(memory_space=pl.ANY)] * 4,
-        out_specs=[pl.BlockSpec(memory_space=pl.ANY)] * 3,
+        out_specs=[pl.BlockSpec(memory_space=pltpu.VMEM)] * 3,
         scratch_shapes=[
             pltpu.VMEM((ROWS, width), F32),
             pltpu.VMEM((ROWS, width), F32),
@@ -380,7 +384,6 @@
             pltpu.VMEM((4 * BLOCKS, QBLOCK), BF16),
             pltpu.VMEM((PACKED, 8 * QBLOCK), BF16),
             pltpu.VMEM((8 * QBLOCK, 1024), BF16),
-            pltpu.VMEM((TOKENS, 512), BF16),
             dma((4,)),
             dma((2,)),
             dma((4,)),
@@ -393,13 +396,22 @@
             dma((2,)),
             dma((7,)),
             dma((8,)),
-            dma((3,)),
         ],
         compiler_params=pltpu.CompilerParams(
-            collective_id=0, has_side_effects=True, vmem_limit_bytes=62 * 2**20
+            collective_id=0, has_side_effects=True, vmem_limit_bytes=40 * 2**20
         ),
         cost_estimate=pl.CostEstimate(flops=2 * 192 * 64 * 8192, bytes_accessed=5 * 2**20, transcendentals=1024),
-    )(inputs, local_weights.reshape(ROWS, width), global_base, momentum)
+    )(inputs, local_weights, global_base, momentum)
+    results = [pltpu.with_memory_space_constraint(a, pltpu.VMEM) for a in results]
+    return pl.pallas_call(
+        store,
+        name="store_results",
+        out_shape=tuple(shape(a.shape, a.dtype) for a in results),
+        in_specs=[pl.BlockSpec(memory_space=pltpu.VMEM)] * 3,
+        out_specs=[pl.BlockSpec(memory_space=pltpu.HBM)] * 3,
+        scratch_shapes=[dma((3,))],
+        compiler_params=pltpu.CompilerParams(vmem_limit_bytes=2 * 2**20),
+    )(*results)
 
 
 def solution(mesh):

time: 58.4 us -> 51 us (0.87); the launches traced: 57.4 us -> 50.9 us
  local copies, waits for them, and re-layouts: 4.95 us -> 0 us
  Pallas kernels: 51.9 us -> 50.2 us
    unnamed x3 -> x0, local copies, waits for them, and re-layouts: 4.95 us -> none
    pallas_call x1 -> x2, Pallas kernels: 51.9 us -> 50.2 us  [the longest x1 49.4 us: shards(): pl.pallas_call(kernel, name='outer_step_and_keys', out_shape=(pltpu.VMEM(...]
where the time goes in v2:
time: 51 us; the launch traced here: 50.9 us
  Pallas kernels  50.2 us (98%)
  between operations  0.64 us (1%)
    pallas_call x1, Pallas kernels, shards(): pl.pallas_call(kernel, name='outer_step_and_keys', out_shape=(pltpu.VMEM(...  49.4 us

profile of v2, /device:TPU:1, one launch (start us, length us, event | category | flops | bytes accessed | tf_op | source)
XLA Modules:
  0.0 50.9 jit_solution(14559689129959724365)
XLA Ops:
  0.6 49.4 %outer_step_and_keys.1 = (f32[8,8192]{1,0:T(8,128)S(1)}, f32[8,8192]{1,0:T(8,128)S(1)}, bf16[192,512]{1,0:T(8,128)(2,1)S(1)}) custom-call(bf16[192,8192]{1,0:T(8,128)(2,1)} %inp.1, f32[8,8192]{1,0:T(8,128)} %bitcast.1, f32[8,8192]{1,0:T(8,128)} %base.1, f32[8,8192]{1,0:T(8,128)} %mom.1), custom_call_target="tpu_custom_call" | custom-call | flops 201326592 | bytes 5242880 | tf_op jit(solution)/shard_map/outer_step_and_keys/pallas_call | solution.py:357
  50.0 0.9 %store_results.1 = (f32[8,8192]{1,0:T(8,128)}, f32[8,8192]{1,0:T(8,128)}, bf16[192,512]{1,0:T(8,128)(2,1)}) custom-call(f32[8,8192]{1,0:T(8,128)S(1)} %get-tuple-element.6.nb, f32[8,8192]{1,0:T(8,128)S(1)} %get-tuple-element.7.nm, bf16[192,512]{1,0:T(8,128)(2,1)S(1)} %get-tuple-element.8.keys), custom_call_target="tpu_custom_call" | custom-call | tf_op jit(solution)/shard_map/store_results/pallas_call | solution.py:406

commit v3 on v2

--- a/solution.py
+++ b/solution.py
@@ -44,7 +44,7 @@
     inp, lw, base, mom, nb_out, nm_out, keys_out,
     lw_v, base_v, mom_v, x_v, spread, core_send, core_recv, far_send, far_recv, lead_send, lead_recv,
     pieces, turned, weight, og_own, og_recv, og_other, part, perm,
-    load_sem, core_sem, far_ssem, far_rsem, lead_sem, piece_ssem, piece_rsem, og_ssem, og_rsem, ogc_sem,
+    load_sem, core_sem, far_ssem, far_rsem, lead_sem, piece_ssem, piece_rsem, near_sem, far_sem, og_ssem, og_rsem, ogc_sem,
     key_ssem, key_rsem,
 ):
     replica = lax.axis_index("replica")
@@ -70,16 +70,18 @@
         pltpu.make_async_copy(mom, mom_v, load_sem.at[2]),
         pltpu.make_async_copy(inp, x_v, load_sem.at[3]),
     ]
-    for load in loads:
-        load.start()
-
     barrier = pltpu.get_barrier_semaphore()
     greeted = 0
 
     def greet(to):
         pl.semaphore_signal(barrier, inc=1, device_id=to, device_id_type=MESH)
 
-    for dz in (6, -6, 2, -2):
+    for dz in (6, -6):
+        greet(at(dz))
+        greeted += 1
+    for load in loads[:2]:
+        load.start()
+    for dz in (2, -2):
         greet(at(dz))
         greeted += 1
     for dx in range(4):
@@ -93,15 +95,20 @@
         for dz in (0, 1, -1, None):
             greet(at(-2 * there if dz is None else -dz, dy))
             greeted += 1
+        for dx in range(1, 4):
+            greet(at(0, dy, dx))
+            greeted += 1
     greet(at(other=True))
     greeted += 1
 
     loads[0].wait()
     loads[1].wait()
+    loads[2].start()
+    loads[3].start()
 
     def quantize(step, carry):
-        for k in range(4):
-            b = step * 4 + k
+        for k in range(16):
+            b = step * 16 + k
             columns = rows(b * QBLOCK, QBLOCK)
             pseudo = base_v[:, columns] - lw_v[:, columns]
             peak = jnp.max(jnp.abs(pseudo), axis=-1, keepdims=True)
@@ -111,7 +118,7 @@
             spread[rows(b * ROWS, ROWS), :] = codes * scale
         return carry
 
-    lax.fori_loop(0, BLOCKS // 4, quantize, 0)
+    lax.fori_loop(0, BLOCKS // 16, quantize, 0)
 
     def row(ref, q):
         return ref[pl.ds(q, BLOCKS, stride=ROWS), :]
@@ -202,41 +209,57 @@
     pieces[place(0, own_slot), :] = new_row[:HALF]
     pieces[place(1, own_slot), :] = new_row[HALF:]
 
-    def send_piece(half, slot, to):
+    def first_path(kind, py, px):
+        return rem(rem(px + py + kind, 4), 3)
+
+    def choose(path, options):
+        return tuple(
+            jnp.where(path == 0, a, jnp.where(path == 1, b, c)) for a, b, c in zip(*options)
+        )
+
+    def send_piece(half, slot, to, sem):
         spot = pieces.at[place(half, slot)]
-        remote(spot, spot, piece_ssem, piece_rsem.at[half * SLOTS + slot], to).start()
-
-    def turn_piece(half, slot):
-        turned[pl.ds(half * HALF * SLOTS + slot, HALF, stride=SLOTS), :] = pieces[
-            place(half, slot), :
-        ].astype(F32)
-
-    def wait_piece(half, slot):
-        spot = pieces.at[place(half, slot)]
-        remote(spot, spot, piece_ssem, piece_rsem.at[half * SLOTS + slot], at(2)).wait_recv()
+        remote(spot, spot, piece_ssem, sem, to).start()
 
     steps = [(a, b) for a in range(4) for b in range(4)]
     length = [0, 1, 2, 1]
     steps.sort(key=lambda s: length[s[0]] + length[s[1]])
+    for a, b in steps[1:]:
+        dz = (0, 1, 2 * mine, -1)[b]
+        options = (at(dz, 0, a), at(dz, a, 0), at(0, a, b))
+        for half in range(2):
+            path = rem(first_path(own_class, y, x) + half, 3)
+            send_piece(half, own_slot, choose(path, options), piece_rsem.at[half * SLOTS + own_slot])
+    og_own[...] = grad.astype(BF16)
+
+    third = (
+        (at(0, 2), at(0, 1), at(0, 3)),
+        (at(0, 0, 2), at(0, 0, 1), at(0, 0, 3)),
+        (at(1), at(-1)),
+    )
+    at_2, at_m2 = at(2), at(-2)
+
     for a, b in steps:
-        dz = (0, 1, 2 * mine, -1)[b]
-        if a or b:
-            send_piece(0, own_slot, at(dz, 0, a))
-            send_piece(1, own_slot, at(dz, a, 0))
-    og_own[...] = grad.astype(BF16)
-
-    for a, b in steps:
-        for half in range(2):
-            px, py = (rem(x + a, 4), y) if half == 0 else (x, rem(y + a, 4))
+        for path in range(3):
+            px = x if path == 1 else rem(x + (a if path == 0 else b), 4)
+            py = y if path == 0 else rem(y + a, 4)
             there = parity(px, py)
-            dz = (0, -1, -2 * there, 1)[b]
+            dz = 0 if path == 2 else (0, -1, -2 * there, 1)[b]
             kind = rem(z + dz + 16 + 2, 4)
             slot = 16 * py + 4 * kind + px
-            if a or b:
-                wait_piece(half, slot)
-            for d in (2, 1, 3):
-                send_piece(half, slot, at(0, d, 0) if half == 0 else at(0, 0, d))
-            turn_piece(half, slot)
+            half = rem(path + 3 - first_path(kind, py, px), 3)
+
+            @pl.when(half < 2)
+            def _(path=path, half=half, slot=slot, there=there, own=not (a or b)):
+                if not own:
+                    spot = pieces.at[place(half, slot)]
+                    remote(spot, spot, piece_ssem, piece_rsem.at[half * SLOTS + slot], at(2)).wait_recv()
+                ends = third[path]
+                if path == 2:
+                    far_end = tuple(jnp.where(there == 1, p, m) for p, m in zip(at_2, at_m2))
+                    ends = (far_end, *ends)
+                for end, sem in zip(ends, (far_sem, near_sem, near_sem)):
+                    send_piece(half, slot, end, sem)
 
     ogs = []
     for j, dz in enumerate((6, -6, 2, -2)):
@@ -246,22 +269,20 @@
         ogs[-1].start()
 
     loads[3].wait()
-    def second(i, carry):
-        kind, p = div(i, 4), rem(i, 4)
-        for d in (1, 3, 2):
-            for half in range(2):
-                if half == 0:
-                    slot = 16 * rem(y + d, 4) + 4 * kind + p
-                else:
-                    slot = 16 * p + 4 * kind + rem(x + d, 4)
-                wait_piece(half, slot)
-                turn_piece(half, slot)
-        return carry
-
-    lax.fori_loop(0, 16, second, 0)
-
-    for b in range(BLOCKS):
-        weight[:, b * QBLOCK : (b + 1) * QBLOCK] = turned[b * SLOTS : (b + 1) * SLOTS, :].astype(BF16)
+    def wait_pieces(count, sem):
+        spots = pieces.at[pl.ds(0, count * HALF)]
+        remote(spots, spots, piece_ssem, sem, at(2)).wait_recv()
+
+    wait_pieces(64, near_sem)
+    wait_pieces(32, far_sem)
+
+    for half in range(2):
+        for slot in range(0, SLOTS, 16):
+            group = pieces[pl.ds((half * SLOTS + slot) * HALF, 16 * HALF), :]
+            group = jnp.transpose(group.reshape(16, HALF, QBLOCK), (1, 0, 2))
+            for b in range(HALF):
+                first = (half * HALF + b) * QBLOCK
+                weight[slot : slot + 16, first : first + QBLOCK] = group[b]
     keys = lax.dot_general(
         x_v[...], weight[...], (((1,), (1,)), ((), ())), preferred_element_type=F32
     ).astype(BF16)
@@ -377,7 +398,7 @@
             pltpu.VMEM((BLOCKS, QBLOCK), F32),
             pltpu.VMEM((BLOCKS, QBLOCK), F32),
             pltpu.VMEM((SLOTS * BLOCKS, QBLOCK), BF16),
-            pltpu.VMEM((SLOTS * BLOCKS, QBLOCK), F32),
+            pltpu.VMEM((BLOCKS * ROWS, QBLOCK), F32),
             pltpu.VMEM((SLOTS, width), BF16),
             pltpu.VMEM((BLOCKS, QBLOCK), BF16),
             pltpu.VMEM((4 * BLOCKS, QBLOCK), BF16),
@@ -391,6 +412,8 @@
             dma((2,)),
             dma,
             dma((2 * SLOTS,)),
+            dma,
+            dma,
             dma((4,)),
             dma((4,)),
             dma((2,)),

time: 51 us -> 48.5 us (0.951)
  Pallas kernels: 50.2 us -> 47.2 us
    pallas_call x1, Pallas kernels: 49.4 us -> 46.4 us  [shards(): pl.pallas_call(kernel, name='outer_step_and_keys', out_shape=(pltpu.VMEM(...]
where the time goes in v3:
time: 48.5 us; the launch traced here: 47.9 us
  Pallas kernels  47.2 us (97%)
  between operations  0.64 us (1%)
    pallas_call x1, Pallas kernels, shards(): pl.pallas_call(kernel, name='outer_step_and_keys', out_shape=(pltpu.VMEM(...  46.4 us

profile of v3, /device:TPU:1, one launch (start us, length us, event | category | flops | bytes accessed | tf_op | source)
XLA Modules:
  0.0 47.9 jit_solution(11704371879264771629)
XLA Ops:
  0.6 46.4 %outer_step_and_keys.1 = (f32[8,8192]{1,0:T(8,128)S(1)}, f32[8,8192]{1,0:T(8,128)S(1)}, bf16[192,512]{1,0:T(8,128)(2,1)S(1)}) custom-call(bf16[192,8192]{1,0:T(8,128)(2,1)} %inp.1, f32[8,8192]{1,0:T(8,128)} %bitcast.1, f32[8,8192]{1,0:T(8,128)} %base.1, f32[8,8192]{1,0:T(8,128)} %mom.1), custom_call_target="tpu_custom_call" | custom-call | flops 201326592 | bytes 5242880 | tf_op jit(solution)/shard_map/outer_step_and_keys/pallas_call | solution.py:378
  47.0 0.9 %store_results.1 = (f32[8,8192]{1,0:T(8,128)}, f32[8,8192]{1,0:T(8,128)}, bf16[192,512]{1,0:T(8,128)(2,1)}) custom-call(f32[8,8192]{1,0:T(8,128)S(1)} %get-tuple-element.6.nb, f32[8,8192]{1,0:T(8,128)S(1)} %get-tuple-element.7.nm, bf16[192,512]{1,0:T(8,128)(2,1)S(1)} %get-tuple-element.8.keys), custom_call_target="tpu_custom_call" | custom-call | tf_op jit(solution)/shard_map/store_results/pallas_call | solution.py:429

commit v4 on v3

--- a/solution.py
+++ b/solution.py
@@ -342,8 +342,9 @@
     early = ordered(0, 6)
     wait_keys(6)
     send_keys(6, 7, at(other=True))
+    early += ordered(6, 7)
     wait_keys(7)
-    done = (early + ordered(6, 8)).astype(BF16)
+    done = (early + ordered(7, 8)).astype(BF16)
     keys_out[:PACKED, :] = done[:, :512]
     keys_out[PACKED:, :] = done[:, 512:]
 

time: 48.5 us -> 48.1 us (level)
  no operation moved by 1% of the time
where the time goes in v4:
time: 48.1 us; the launch traced here: 47.5 us
  Pallas kernels  46.9 us (98%)
  between operations  0.64 us (1%)
    pallas_call x1, Pallas kernels, shards(): pl.pallas_call(kernel, name='outer_step_and_keys', out_shape=(pltpu.VMEM(...  46 us

profile of v4, /device:TPU:1, one launch (start us, length us, event | category | flops | bytes accessed | tf_op | source)
XLA Modules:
  0.0 47.5 jit_solution(8515775889667525438)
XLA Ops:
  0.6 46.0 %outer_step_and_keys.1 = (f32[8,8192]{1,0:T(8,128)S(1)}, f32[8,8192]{1,0:T(8,128)S(1)}, bf16[192,512]{1,0:T(8,128)(2,1)S(1)}) custom-call(bf16[192,8192]{1,0:T(8,128)(2,1)} %inp.1, f32[8,8192]{1,0:T(8,128)} %bitcast.1, f32[8,8192]{1,0:T(8,128)} %base.1, f32[8,8192]{1,0:T(8,128)} %mom.1), custom_call_target="tpu_custom_call" | custom-call | flops 201326592 | bytes 5242880 | tf_op jit(solution)/shard_map/outer_step_and_keys/pallas_call | solution.py:379
  46.6 0.9 %store_results.1 = (f32[8,8192]{1,0:T(8,128)}, f32[8,8192]{1,0:T(8,128)}, bf16[192,512]{1,0:T(8,128)(2,1)}) custom-call(f32[8,8192]{1,0:T(8,128)S(1)} %get-tuple-element.6.nb, f32[8,8192]{1,0:T(8,128)S(1)} %get-tuple-element.7.nm, bf16[192,512]{1,0:T(8,128)(2,1)S(1)} %get-tuple-element.8.keys), custom_call_target="tpu_custom_call" | custom-call | tf_op jit(solution)/shard_map/store_results/pallas_call | solution.py:430
